TPU v7x, 512 devices: a whole 4x8x8 slice. The times are simulated.
512 devices in a mesh: row: 64 (over y, z), col: 8 (over x, core).
Axes of the slice: x: 4, y: 8, z: 8, core: 2. Of those that a mesh axis runs over, the one named last changes fastest.
Arguments:
- features: bfloat16 [65536, 512], P(('row', 'col')), may hold values from -6 to 6
- weight: bfloat16 [512, 512], replicated, may hold values from -0.25 to 0.25
- bias_vec: float32 [512], replicated, may hold values from -3 to 3
- tile_vals: bfloat16 [64, 8, 16, 128, 128], P('row', 'col'), may hold values from -0.1875 to 0.1875
- tile_coords: int32 [64, 8, 16, 2], P('row', 'col'), may hold values from 0 to 63, as said below
- tile_count: int32 [64, 8], P('row', 'col'), may hold values from 2 to 16, as said below
- cotangent: bfloat16 [65536, 512], P(('row', 'col')), may hold values from -6 to 6
Outputs:
- layer_out: bfloat16 [65536, 512], P(('row', 'col'))
- grad_weight: float32 [512, 512], replicated
- grad_bias: float32 [512], replicated
- grad_features: bfloat16 [65536, 512], P(('row', 'col'))
Inputs may be any that keep to these rules, and one draw needn't show every extreme that they name: tile_coords[r, c, s, 0] is below 8; tile_coords[r, c, s, 1] lies in the row bands r - 3 to r + 3 that exist. `tile_count`: some device has all 16 slots live.
All inputs are finite; a program needn't handle non-finite values.
Results may differ from a plain program's by a relative error of at most 0.019.
Values may be sent and summed in bfloat16 or wider, within the bound.
No kernel may reach another device: no remote copies, remote signals or barrier semaphores. Data moves between devices by JAX's collectives and lax.ppermute only.
A program may use at most 64 MiB of HBM per device.

v0:
```python
import jax
import jax.numpy as jnp
from jax import lax
from jax.sharding import PartitionSpec as P

REACH = 3


def passed_along(block, axis, distance):
    devices = range(lax.axis_size(axis))
    route = [(i - distance, i) for i in devices if i - distance in devices]
    return lax.ppermute(block, axis, route)


def gelu_tanh(values):
    return jax.nn.gelu(values, approximate=True)


def body(features, weight, bias_vec, tile_vals, tile_coords, tile_count, cotangent):
    col_count = lax.axis_size("col")
    own_row = lax.axis_index("row")
    tiles_here = tile_vals[0, 0]
    coords_here = tile_coords[0, 0]
    live_count = tile_count[0, 0]
    slot_count = tiles_here.shape[0]
    tile_size = features.shape[0]
    feat_width = features.shape[1]
    window = 2 * REACH + 1
    per_step = 8
    row_local = coords_here[:, 0]
    col_local = coords_here[:, 1]
    alive_mask = (jnp.arange(slot_count, dtype=jnp.int32) < live_count).astype(jnp.float32)
    window_index = col_local - own_row + REACH
    nearby = []
    for shift_by in range(-REACH, REACH + 1):
        if shift_by == 0:
            nearby.append(features)
        else:
            nearby.append(passed_along(features, "row", -shift_by))
    panels = jnp.stack(nearby)
    step_total = slot_count // per_step

    def slot_slices(group_idx):
        first_slot = group_idx * per_step
        tiles_now = lax.dynamic_slice_in_dim(tiles_here, first_slot, per_step, 0)
        alive_now = lax.dynamic_slice_in_dim(alive_mask, first_slot, per_step, 0)
        return (first_slot, tiles_now, alive_now)

    def forward_group(group_idx, totals):
        first_slot, tiles_now, alive_now = slot_slices(group_idx)
        col_pick = lax.dynamic_slice_in_dim(window_index, first_slot, per_step, 0)
        row_pick = lax.dynamic_slice_in_dim(row_local, first_slot, per_step, 0)
        picked = panels[col_pick]
        product = jnp.einsum("gij,gjf->gif", tiles_now, picked, preferred_element_type=jnp.float32)
        onehot = (row_pick[:, None] == jnp.arange(col_count, dtype=jnp.int32)[None, :]).astype(
            jnp.float32
        )
        onehot = onehot * alive_now[:, None]
        return totals + jnp.einsum("gb,gif->bif", onehot, product)

    partial_value = lax.fori_loop(
        0, step_total, forward_group, jnp.zeros((col_count, tile_size, feat_width), jnp.float32)
    )
    aggregate = lax.psum_scatter(
        partial_value.reshape(col_count * tile_size, feat_width),
        "col",
        scatter_dimension=0,
        tiled=True,
    )
    aggregate_b = aggregate.astype(jnp.bfloat16)
    pre_act = jnp.dot(aggregate_b, weight, preferred_element_type=jnp.float32) + bias_vec
    layer_out = gelu_tanh(pre_act).astype(jnp.bfloat16)
    unused_out, pullback = jax.vjp(gelu_tanh, pre_act)
    grad_pre = pullback(cotangent.astype(jnp.float32))[0].astype(jnp.bfloat16)
    weight_term = jnp.einsum("nf,ng->fg", aggregate_b, grad_pre, preferred_element_type=jnp.float32)
    bias_term = jnp.sum(grad_pre.astype(jnp.float32), axis=0)
    grad_weight, grad_bias = lax.psum((weight_term, bias_term), ("row", "col"))
    grad_mid = jnp.einsum("ng,fg->nf", grad_pre, weight, preferred_element_type=jnp.float32).astype(
        jnp.bfloat16
    )
    band_panels = lax.all_gather(grad_mid, "col", axis=0, tiled=True).reshape(
        col_count, tile_size, feat_width
    )

    def backward_group(group_idx, totals):
        first_slot, tiles_now, alive_now = slot_slices(group_idx)
        row_pick = lax.dynamic_slice_in_dim(row_local, first_slot, per_step, 0)
        win_pick = lax.dynamic_slice_in_dim(window_index, first_slot, per_step, 0)
        picked = band_panels[row_pick]
        product = jnp.einsum("gji,gjf->gif", tiles_now, picked, preferred_element_type=jnp.float32)
        onehot = (win_pick[:, None] == jnp.arange(window, dtype=jnp.int32)[None, :]).astype(
            jnp.float32
        )
        onehot = onehot * alive_now[:, None]
        return totals + jnp.einsum("gb,gif->bif", onehot, product)

    grad_acc = lax.fori_loop(
        0, step_total, backward_group, jnp.zeros((window, tile_size, feat_width), jnp.float32)
    )
    result_sum = grad_acc[REACH]
    for shift_by in range(-REACH, REACH + 1):
        if shift_by != 0:
            result_sum = result_sum + passed_along(grad_acc[shift_by + REACH], "row", shift_by)
    grad_features = result_sum.astype(jnp.bfloat16)
    return (layer_out, grad_weight, grad_bias, grad_features)


def solution(mesh):
    return jax.shard_map(
        body,
        mesh=mesh,
        in_specs=(
            P(("row", "col"), None),
            P(),
            P(),
            P("row", "col", None, None, None),
            P("row", "col", None, None),
            P("row", "col"),
            P(("row", "col"), None),
        ),
        out_specs=(P(("row", "col"), None), P(), P(), P(("row", "col"), None)),
        check_vma=False,
    )
```

profile of v0, /device:TPU:24, one launch (start us, length us, event | category | flops | bytes accessed | tf_op | source)
XLA Modules:
  0.0 473.3 jit_solution(12974934062237815644)
XLA Ops:
  7.2 8.0 %collective-permute-start = (bf16[128,512]{1,0:T(8,128)(2,1)}, bf16[128,512]{1,0:T(8,128)(2,1)S(1)}, u32[]{:S(2)}, u32[]{:S(2)}) collective-permute-start(bf16[128,512]{1,0:T(8,128)(2,1)} %param.11), channel_id=1, source_target_pairs={{0,24},{8,32},{16,40},{24,48},{32,56},{40,64},{48,72},{56,80},{64,... | collective-permute-start | bytes 393224 | tf_op jit(solution)/shard_map/ppermute | solution.py:12
  15.3 6.4 %collective-permute-start.1 = (bf16[128,512]{1,0:T(8,128)(2,1)}, bf16[128,512]{1,0:T(8,128)(2,1)S(1)}, u32[]{:S(2)}, u32[]{:S(2)}) collective-permute-start(bf16[128,512]{1,0:T(8,128)(2,1)} %param.11), channel_id=1, source_target_pairs={{0,16},{8,24},{16,32},{24,40},{32,48},{40,56},{48,64},{56,72},{64,... | collective-permute-start | bytes 393224 | tf_op jit(solution)/shard_map/ppermute | solution.py:12
  21.7 3.4 collective-permute-start.2
  25.1 4.6 collective-permute-start.3
  29.6 1.9 collective-permute-start.4
  33.0 4.2 collective-permute-start.5
  38.2 2.6 collective-permute-done.4
  40.9 11.6 %collective-permute-done.5 = bf16[128,512]{1,0:T(8,128)(2,1)S(1)} collective-permute-done((bf16[128,512]{1,0:T(8,128)(2,1)}, bf16[128,512]{1,0:T(8,128)(2,1)S(1)}, u32[]{:S(2)}, u32[]{:S(2)}) %collective-permute-start.5) | collective-permute-done | bytes 131104 | tf_op jit(solution)/shard_map/ppermute | solution.py:12
  52.5 10.2 %while.28 = (s32[]{:T(128)}, f32[8,128,512]{2,0,1:T(8,128)}, s32[16]{0:T(128)S(1)}, bf16[16]{0:T(256)(128)(2,1)S(1)}, bf16[16,128,128]{2,1,0:T(8,128)(2,1)}, /*i...) while((s32[]{:T(128)}, f32[8,128,512]{2,0,1:T(8,128)}, ...), condition=%wide.region_1.0_spmd.clone, body=%wide.region_0.0_spmd.clone.sunk | while | flops 143656096 | bytes 9703877 | solution.py:61
  54.7 2.1 select_add_fusion.4
  59.1 3.7 select_add_fusion.4
  62.7 4.1 copy.18
  67.0 33.2 %reduce-scatter.2.cloned.1.call-done = f32[128,512]{1,0:T(8,128)} async-done(((f32[1024,512]{1,0:T(8,128)}), f32[128,512]{1,0:T(8,128)}) %reduce-scatter.2.cloned.1.call-update) | async-done | bytes 262160 | tf_op jit(solution)/shard_map/reduce_scatter | solution.py:64
  100.2 2.0 convert_reduce_fusion
  103.2 27.5 %all-gather.2.cloned.1.call-done = bf16[1024,512]{1,0:T(8,128)(2,1)} async-done(((bf16[128,512]{1,0:T(8,128)(2,1)}), bf16[1024,512]{1,0:T(8,128)(2,1)}) %all-gather.2.cloned.1.call-update) | async-done | bytes 1048592 | tf_op jit(solution)/shard_map/all_gather | solution.py:81
  130.8 11.0 %while.29 = (s32[]{:T(128)}, f32[7,128,512]{2,0,1:T(8,128)}, s32[16]{0:T(128)S(1)}, bf16[16]{0:T(256)(128)(2,1)S(1)}, bf16[16,128,128]{2,1,0:T(8,128)(2,1)S(1)},...) while((s32[]{:T(128)}, f32[7,128,512]{2,0,1:T(8,128)}, ...), condition=%wide.region_7.0_spmd.clone, body=%wide.region_6.0_spmd.clone.sunk | while | flops 142476432 | bytes 9179589 | solution.py:97
  130.9 1.8 gather_fusion.1
  133.4 2.1 select_add_fusion.5
  135.6 1.8 gather_fusion.1
  138.1 3.7 select_add_fusion.5
  141.8 2.7 copy.19
  145.4 4.6 collective-permute-start.10
  150.1 6.0 %collective-permute-start.11 = (f32[128,512]{1,0:T(8,128)}, f32[128,512]{1,0:T(8,128)S(1)}, u32[]{:S(2)}, u32[]{:S(2)}) collective-permute-start(f32[128,512]{1,0:T(8,128)} %get-tuple-element.333), channel_id=1, source_target_pairs={{0,24},{8,32},{16,40},{24,48},{32,56},{40,64},{48,72},{56,80},{64,... | collective-permute-start | bytes 786440 | tf_op jit(solution)/shard_map/ppermute | solution.py:12
  156.1 3.7 collective-permute-start.6
  159.8 3.3 collective-permute-start.7
  163.2 3.7 collective-permute-start.8
  166.9 1.6 collective-permute-done.10
  168.5 3.8 collective-permute-start.9
  173.7 123.1 %psum.15 = f32[512]{0:T(512)} all-reduce(f32[512]{0:T(512)S(1)} %get-tuple-element.330), channel_id=1, replica_groups=mesh['row'=64,'col'=8] {'row','col'}, use_global_device_ids=true, to_apply=%region_5.0 | all-reduce | flops 512 | bytes 4096 | tf_op jit(solution)/shard_map/psum | solution.py:77
  296.9 2.0 fusion.42
  298.9 165.6 %all-reduce.2.cloned.1.call-done = f32[512,512]{1,0:T(8,128)} async-done(((f32[512,512]{1,0:T(8,128)}), f32[512,512]{1,0:T(8,128)}) %all-reduce.2.cloned.1.call-update) | async-done | bytes 1048592 | tf_op jit(solution)/shard_map/psum | solution.py:77
  464.5 2.3 copy.60
  (61 shorter events, 11.1 us)
Async XLA Ops:
  7.2 93.0 %copy-start = (bf16[512,512]{1,0:T(8,128)(2,1)S(1)}, bf16[512,512]{1,0:T(8,128)(2,1)}, u32[]{:S(2)}) copy-start(bf16[512,512]{1,0:T(8,128)(2,1)} %param.12) | copy-start | bytes 1572868
  7.2 93.0 %reduce-scatter.2.cloned.1.call-start = ((), (), s32[]{:S(2)}) async-start(), calls=%async_computation.1 | async-start | bytes 2359296 | tf_op jit(solution)/shard_map/reduce_scatter | solution.py:64
  7.2 25.8 %collective-permute-start = (bf16[128,512]{1,0:T(8,128)(2,1)}, bf16[128,512]{1,0:T(8,128)(2,1)S(1)}, u32[]{:S(2)}, u32[]{:S(2)}) collective-permute-start(bf16[128,512]{1,0:T(8,128)(2,1)} %param.11), channel_id=1, source_target_pairs={{0,24},{8,32},{16,40},{24,48},{32,56},{40,64},{48,72},{56,80},{64,... | collective-permute-start | bytes 393224 | tf_op jit(solution)/shard_map/ppermute | solution.py:12
  15.3 22.0 %collective-permute-start.1 = (bf16[128,512]{1,0:T(8,128)(2,1)}, bf16[128,512]{1,0:T(8,128)(2,1)S(1)}, u32[]{:S(2)}, u32[]{:S(2)}) collective-permute-start(bf16[128,512]{1,0:T(8,128)(2,1)} %param.11), channel_id=1, source_target_pairs={{0,16},{8,24},{16,32},{24,40},{32,48},{40,56},{48,64},{56,72},{64,... | collective-permute-start | bytes 393224 | tf_op jit(solution)/shard_map/ppermute | solution.py:12
  21.7 15.6 %collective-permute-start.2 = (bf16[128,512]{1,0:T(8,128)(2,1)}, bf16[128,512]{1,0:T(8,128)(2,1)S(1)}, u32[]{:S(2)}, u32[]{:S(2)}) collective-permute-start(bf16[128,512]{1,0:T(8,128)(2,1)} %param.11), channel_id=1, source_target_pairs={{0,8},{8,16},{16,24},{24,32},{32,40},{40,48},{48,56},{56,64},{64,7... | collective-permute-start | bytes 393224 | tf_op jit(solution)/shard_map/ppermute | solution.py:12
  25.1 13.1 %collective-permute-start.3 = (bf16[128,512]{1,0:T(8,128)(2,1)}, bf16[128,512]{1,0:T(8,128)(2,1)S(1)}, u32[]{:S(2)}, u32[]{:S(2)}) collective-permute-start(bf16[128,512]{1,0:T(8,128)(2,1)} %param.11), channel_id=1, source_target_pairs={{8,0},{16,8},{24,16},{32,24},{40,32},{48,40},{56,48},{64,56},{72,6... | collective-permute-start | bytes 393224 | tf_op jit(solution)/shard_map/ppermute | solution.py:12
  29.6 11.2 %collective-permute-start.4 = (bf16[128,512]{1,0:T(8,128)(2,1)}, bf16[128,512]{1,0:T(8,128)(2,1)S(1)}, u32[]{:S(2)}, u32[]{:S(2)}) collective-permute-start(bf16[128,512]{1,0:T(8,128)(2,1)} %param.11), channel_id=1, source_target_pairs={{16,0},{24,8},{32,16},{40,24},{48,32},{56,40},{64,48},{72,56},{80,... | collective-permute-start | bytes 393224 | tf_op jit(solution)/shard_map/ppermute | solution.py:12
  33.0 19.5 %collective-permute-start.5 = (bf16[128,512]{1,0:T(8,128)(2,1)}, bf16[128,512]{1,0:T(8,128)(2,1)S(1)}, u32[]{:S(2)}, u32[]{:S(2)}) collective-permute-start(bf16[128,512]{1,0:T(8,128)(2,1)} %param.11), channel_id=1, source_target_pairs={{24,0},{32,8},{40,16},{48,24},{56,32},{64,40},{72,48},{80,56},{88,... | collective-permute-start | bytes 393224 | tf_op jit(solution)/shard_map/ppermute | solution.py:12
  66.9 33.3 %copy-start.3 = (bf16[128,512]{1,0:T(8,128)(2,1)S(1)}, bf16[128,512]{1,0:T(8,128)(2,1)}, u32[]{:S(2)}) copy-start(bf16[128,512]{1,0:T(8,128)(2,1)} %param.17) | copy-start | bytes 393220
  66.9 33.3 %copy-start.4 = (f32[512]{0:T(512)S(1)}, f32[512]{0:T(512)}, u32[]{:S(2)}) copy-start(f32[512]{0:T(512)} %param.13) | copy-start | bytes 6148
  66.9 63.9 %copy-start.1 = (bf16[16,128,128]{2,1,0:T(8,128)(2,1)S(1)}, bf16[16,128,128]{2,1,0:T(8,128)(2,1)}, u32[]{:S(2)}) copy-start(bf16[16,128,128]{2,1,0:T(8,128)(2,1)} %get-tuple-element.501) | copy-start | bytes 1572868
  66.9 63.9 %all-gather.2.cloned.1.call-start = ((), (), s32[]{:S(2)}) async-start(), calls=%async_computation.3 | async-start | bytes 1179648 | tf_op jit(solution)/shard_map/all_gather | solution.py:81
  103.2 361.3 %all-reduce.2.cloned.1.call-start = ((), (), s32[]{:S(2)}) async-start(), calls=%async_computation.2 | async-start | bytes 2097152 | tf_op jit(solution)/shard_map/psum | solution.py:77
  144.5 27.9 %copy-start.2 = (f32[128,512]{1,0:T(8,128)S(1)}, f32[128,512]{1,0:T(8,128)}, u32[]{:S(2)}) copy-start(f32[128,512]{1,0:T(8,128)} %reduce-scatter.2.cloned.1.call-done) | copy-start | bytes 786436
  145.4 23.1 %collective-permute-start.10 = (f32[128,512]{1,0:T(8,128)S(1)}, f32[128,512]{1,0:T(8,128)S(1)}, u32[]{:S(2)}, u32[]{:S(2)}) collective-permute-start(f32[128,512]{1,0:T(8,128)S(1)} %get-tuple-element.334), channel_id=1, source_target_pairs={{0,16},{8,24},{16,32},{24,40},{32,48},{40,56},{48,64},{56,72},{64,... | collective-permute-start | bytes 786440 | tf_op jit(solution)/shard_map/ppermute | solution.py:12
  150.1 146.8 %collective-permute-start.11 = (f32[128,512]{1,0:T(8,128)}, f32[128,512]{1,0:T(8,128)S(1)}, u32[]{:S(2)}, u32[]{:S(2)}) collective-permute-start(f32[128,512]{1,0:T(8,128)} %get-tuple-element.333), channel_id=1, source_target_pairs={{0,24},{8,32},{16,40},{24,48},{32,56},{40,64},{48,72},{56,80},{64,... | collective-permute-start | bytes 786440 | tf_op jit(solution)/shard_map/ppermute | solution.py:12
  156.1 140.7 %collective-permute-start.6 = (f32[128,512]{1,0:T(8,128)}, f32[128,512]{1,0:T(8,128)}, u32[]{:S(2)}, u32[]{:S(2)}) collective-permute-start(f32[128,512]{1,0:T(8,128)} %get-tuple-element.332), channel_id=1, source_target_pairs={{24,0},{32,8},{40,16},{48,24},{56,32},{64,40},{72,48},{80,56},{88,... | collective-permute-start | bytes 786440 | tf_op jit(solution)/shard_map/ppermute | solution.py:12
  159.8 137.0 %collective-permute-start.7 = (f32[128,512]{1,0:T(8,128)}, f32[128,512]{1,0:T(8,128)}, u32[]{:S(2)}, u32[]{:S(2)}) collective-permute-start(f32[128,512]{1,0:T(8,128)} %get-tuple-element.337), channel_id=1, source_target_pairs={{16,0},{24,8},{32,16},{40,24},{48,32},{56,40},{64,48},{72,56},{80,... | collective-permute-start | bytes 786440 | tf_op jit(solution)/shard_map/ppermute | solution.py:12
  163.2 133.7 %collective-permute-start.8 = (f32[128,512]{1,0:T(8,128)S(1)}, f32[128,512]{1,0:T(8,128)}, u32[]{:S(2)}, u32[]{:S(2)}) collective-permute-start(f32[128,512]{1,0:T(8,128)S(1)} %get-tuple-element.336), channel_id=1, source_target_pairs={{8,0},{16,8},{24,16},{32,24},{40,32},{48,40},{56,48},{64,56},{72,6... | collective-permute-start | bytes 786440 | tf_op jit(solution)/shard_map/ppermute | solution.py:12
  168.5 128.3 %collective-permute-start.9 = (f32[128,512]{1,0:T(8,128)S(1)}, f32[128,512]{1,0:T(8,128)}, u32[]{:S(2)}, u32[]{:S(2)}) collective-permute-start(f32[128,512]{1,0:T(8,128)S(1)} %get-tuple-element.335), channel_id=1, source_target_pairs={{0,8},{8,16},{16,24},{24,32},{32,40},{40,48},{48,56},{56,64},{64,7... | collective-permute-start | bytes 786440 | tf_op jit(solution)/shard_map/ppermute | solution.py:12
Sparse Core Ops, SparseCore 0:
  67.0 33.0 reduce-scatter.1
  103.3 27.4 all-gather.1
  173.8 290.6 all-reduce.1
where the time goes:
time: 474 us; the launch traced here: 473 us
  waiting for transfers between devices  242 us (51%)
  blocking collectives  123 us (26%)
  starting transfers between devices  53.9 us (11%)
  matrix products  19.6 us (4%)
  local copies, waits for them, and re-layouts  16.5 us (3%)
  between operations  14.6 us (3%)
    psum x1, waiting for transfers between devices, body(): grad_weight, grad_bias = lax.psum((weight_term, bias_term), ('row', 'col'))  166 us
    psum x1, blocking collectives, body(): grad_weight, grad_bias = lax.psum((weight_term, bias_term), ('row', 'col'))  123 us
    ppermute x12, starting transfers between devices, passed_along(): return lax.ppermute(block, axis, route)  53.8 us
    reduce_scatter x1, waiting for transfers between devices, body(): lax.psum_scatter(partial_value.reshape(col_count * tile_size, feat_width)...  33.2 us
    all_gather x1, waiting for transfers between devices, body(): lax.all_gather(grad_mid, 'col', axis=0, tiled=True)  27.5 us
    ppermute x12, waiting for transfers between devices, passed_along(): return lax.ppermute(block, axis, route)  15.9 us
  transfers between devices with their start and end apart: 15, of which 6 were waited for; matrix products, arithmetic and copies ran while one was open for 1% of the time, Pallas kernels for 0%

commit v1 on v0

--- a/solution.py
+++ b/solution.py
@@ -74,7 +74,7 @@
     grad_pre = pullback(cotangent.astype(jnp.float32))[0].astype(jnp.bfloat16)
     weight_term = jnp.einsum("nf,ng->fg", aggregate_b, grad_pre, preferred_element_type=jnp.float32)
     bias_term = jnp.sum(grad_pre.astype(jnp.float32), axis=0)
-    grad_weight, grad_bias = lax.psum((weight_term, bias_term), ("row", "col"))
+    grad_weight, grad_bias = lax.psum(lax.psum((weight_term, bias_term), "row"), "col")
     grad_mid = jnp.einsum("ng,fg->nf", grad_pre, weight, preferred_element_type=jnp.float32).astype(
         jnp.bfloat16
     )

time: 474 us -> 501 us (1.057)
  the two profiles are of different devices: /device:TPU:24 before, /device:TPU:1 now
where the time goes in v1:
time: 501 us; the launch traced here: 500 us
  waiting for transfers between devices  239 us (48%)
  blocking collectives  158 us (32%)
  starting transfers between devices  48.8 us (10%)
  matrix products  19.7 us (4%)
  local copies, waits for them, and re-layouts  16.6 us (3%)
  between operations  14.7 us (3%)
    psum x1, waiting for transfers between devices, body(): lax.psum((weight_term, bias_term), 'row')  157 us
    psum x1, blocking collectives, body(): lax.psum((weight_term, bias_term), 'row')  113 us
    ppermute x12, starting transfers between devices, passed_along(): return lax.ppermute(block, axis, route)  48.7 us
    psum x1, blocking collectives, body(): lax.psum(lax.psum((weight_term, bias_term), 'row'), 'col')  44.8 us
    reduce_scatter x1, waiting for transfers between devices, body(): lax.psum_scatter(partial_value.reshape(col_count * tile_size, feat_width)...  34.3 us
    all_gather x1, waiting for transfers between devices, body(): lax.all_gather(grad_mid, 'col', axis=0, tiled=True)  28.7 us
    ppermute x12, waiting for transfers between devices, passed_along(): return lax.ppermute(block, axis, route)  19.3 us
  transfers between devices with their start and end apart: 16, of which 5 were waited for; matrix products, arithmetic and copies ran while one was open for 4% of the time, Pallas kernels for 0%

profile of v1, /device:TPU:1, one launch (start us, length us, event | category | flops | bytes accessed | tf_op | source)
XLA Modules:
  0.0 500.0 jit_solution(13246829573797859506)
XLA Ops:
  7.2 8.6 %collective-permute-start = (bf16[128,512]{1,0:T(8,128)(2,1)}, bf16[128,512]{1,0:T(8,128)(2,1)S(1)}, u32[]{:S(2)}, u32[]{:S(2)}) collective-permute-start(bf16[128,512]{1,0:T(8,128)(2,1)} %param.11), channel_id=1, source_target_pairs={{0,24},{8,32},{16,40},{24,48},{32,56},{40,64},{48,72},{56,80},{64,... | collective-permute-start | bytes 393224 | tf_op jit(solution)/shard_map/ppermute | solution.py:12
  15.8 6.1 %collective-permute-start.1 = (bf16[128,512]{1,0:T(8,128)(2,1)}, bf16[128,512]{1,0:T(8,128)(2,1)S(1)}, u32[]{:S(2)}, u32[]{:S(2)}) collective-permute-start(bf16[128,512]{1,0:T(8,128)(2,1)} %param.11), channel_id=1, source_target_pairs={{0,16},{8,24},{16,32},{24,40},{32,48},{40,56},{48,64},{56,72},{64,... | collective-permute-start | bytes 393224 | tf_op jit(solution)/shard_map/ppermute | solution.py:12
  22.0 3.1 collective-permute-start.2
  25.1 1.3 collective-permute-start.3
  26.4 1.3 collective-permute-start.4
  31.4 6.2 %collective-permute-done.4 = bf16[128,512]{1,0:T(8,128)(2,1)S(1)} collective-permute-done((bf16[128,512]{1,0:T(8,128)(2,1)}, bf16[128,512]{1,0:T(8,128)(2,1)S(1)}, u32[]{:S(2)}, u32[]{:S(2)}) %collective-permute-start.4) | collective-permute-done | bytes 131104 | tf_op jit(solution)/shard_map/ppermute | solution.py:12
  37.6 13.1 %collective-permute-done.5 = bf16[128,512]{1,0:T(8,128)(2,1)S(1)} collective-permute-done((bf16[128,512]{1,0:T(8,128)(2,1)}, bf16[128,512]{1,0:T(8,128)(2,1)S(1)}, u32[]{:S(2)}, u32[]{:S(2)}) %collective-permute-start.5) | collective-permute-done | bytes 131104 | tf_op jit(solution)/shard_map/ppermute | solution.py:12
  50.7 10.3 %while.28 = (s32[]{:T(128)}, f32[8,128,512]{2,0,1:T(8,128)}, s32[16]{0:T(128)S(1)}, bf16[16]{0:T(256)(128)(2,1)S(1)}, bf16[16,128,128]{2,1,0:T(8,128)(2,1)}, /*i...) while((s32[]{:T(128)}, f32[8,128,512]{2,0,1:T(8,128)}, ...), condition=%wide.region_1.0_spmd.clone, body=%wide.region_0.0_spmd.clone.sunk | while | flops 143656096 | bytes 9703877 | solution.py:61
  51.4 1.4 fusion.67
  53.0 2.1 select_add_fusion.4
  55.8 1.4 fusion.67
  57.3 3.7 select_add_fusion.4
  61.0 4.1 copy.18
  65.2 34.3 %reduce-scatter.2.cloned.1.call-done = f32[128,512]{1,0:T(8,128)} async-done(((f32[1024,512]{1,0:T(8,128)}), f32[128,512]{1,0:T(8,128)}) %reduce-scatter.2.cloned.1.call-update) | async-done | bytes 262160 | tf_op jit(solution)/shard_map/reduce_scatter | solution.py:64
  99.5 2.1 convert_reduce_fusion
  102.6 1.3 fusion.43
  104.0 28.7 %all-gather.2.cloned.1.call-done = bf16[1024,512]{1,0:T(8,128)(2,1)} async-done(((bf16[128,512]{1,0:T(8,128)(2,1)}), bf16[1024,512]{1,0:T(8,128)(2,1)}) %all-gather.2.cloned.1.call-update) | async-done | bytes 1048592 | tf_op jit(solution)/shard_map/all_gather | solution.py:81
  132.7 11.0 %while.29 = (s32[]{:T(128)}, f32[7,128,512]{2,0,1:T(8,128)}, s32[16]{0:T(128)S(1)}, bf16[16]{0:T(256)(128)(2,1)S(1)}, bf16[16,128,128]{2,1,0:T(8,128)(2,1)S(1)},...) while((s32[]{:T(128)}, f32[7,128,512]{2,0,1:T(8,128)}, ...), condition=%wide.region_9.0_spmd.clone, body=%wide.region_8.0_spmd.clone.sunk | while | flops 142476432 | bytes 9179589 | solution.py:97
  132.8 1.8 gather_fusion.1
  135.2 2.1 select_add_fusion.5
  137.5 1.8 gather_fusion.1
  140.0 3.7 select_add_fusion.5
  143.7 2.7 copy.19
  147.3 4.2 collective-permute-start.10
  151.5 5.7 %collective-permute-start.11 = (f32[128,512]{1,0:T(8,128)}, f32[128,512]{1,0:T(8,128)S(1)}, u32[]{:S(2)}, u32[]{:S(2)}) collective-permute-start(f32[128,512]{1,0:T(8,128)} %get-tuple-element.333), channel_id=1, source_target_pairs={{0,24},{8,32},{16,40},{24,48},{32,56},{40,64},{48,72},{56,80},{64,... | collective-permute-start | bytes 786440 | tf_op jit(solution)/shard_map/ppermute | solution.py:12
  157.3 1.3 collective-permute-start.6
  161.2 13.2 %collective-permute-start.9 = (f32[128,512]{1,0:T(8,128)S(1)}, f32[128,512]{1,0:T(8,128)}, u32[]{:S(2)}, u32[]{:S(2)}) collective-permute-start(f32[128,512]{1,0:T(8,128)S(1)} %get-tuple-element.335), channel_id=1, source_target_pairs={{0,8},{8,16},{16,24},{24,32},{32,40},{40,48},{48,56},{56,64},{64,7... | collective-permute-start | bytes 786440 | tf_op jit(solution)/shard_map/ppermute | solution.py:12
  174.3 156.8 %all-reduce.3.cloned.1.call-done = f32[512,512]{1,0:T(8,128)} async-done(((f32[512,512]{1,0:T(8,128)}), f32[512,512]{1,0:T(8,128)}) %all-reduce.3.cloned.1.call-update) | async-done | bytes 1048592 | tf_op jit(solution)/shard_map/psum | solution.py:77
  331.1 113.3 %psum.30 = f32[512]{0:T(512)S(1)} all-reduce(f32[512]{0:T(512)S(1)} %get-tuple-element.330), channel_id=1, replica_groups=mesh['row'=64,'col'=8] {'row'}, use_global_device_ids=true, to_apply=%region_6.0 | all-reduce | flops 512 | bytes 4096 | tf_op jit(solution)/shard_map/psum | solution.py:77
  444.5 44.8 %psum.31 = f32[512]{0:T(512)} all-reduce(f32[512]{0:T(512)S(1)} %psum.30), channel_id=1, replica_groups=mesh['row'=64,'col'=8] {'col'}, use_global_device_ids=true, to_apply=%region_7.0 | all-reduce | flops 512 | bytes 4096 | tf_op jit(solution)/shard_map/psum | solution.py:77
  489.3 2.0 fusion.42
  491.2 2.3 copy.61
  (65 shorter events, 11.0 us)
Async XLA Ops:
  7.2 92.3 %copy-start = (bf16[512,512]{1,0:T(8,128)(2,1)S(1)}, bf16[512,512]{1,0:T(8,128)(2,1)}, u32[]{:S(2)}) copy-start(bf16[512,512]{1,0:T(8,128)(2,1)} %param.12) | copy-start | bytes 1572868
  7.2 92.3 %reduce-scatter.2.cloned.1.call-start = ((), (), s32[]{:S(2)}) async-start(), calls=%async_computation.1 | async-start | bytes 2359296 | tf_op jit(solution)/shard_map/reduce_scatter | solution.py:64
  7.2 21.9 %collective-permute-start = (bf16[128,512]{1,0:T(8,128)(2,1)}, bf16[128,512]{1,0:T(8,128)(2,1)S(1)}, u32[]{:S(2)}, u32[]{:S(2)}) collective-permute-start(bf16[128,512]{1,0:T(8,128)(2,1)} %param.11), channel_id=1, source_target_pairs={{0,24},{8,32},{16,40},{24,48},{32,56},{40,64},{48,72},{56,80},{64,... | collective-permute-start | bytes 393224 | tf_op jit(solution)/shard_map/ppermute | solution.py:12
  15.8 14.6 %collective-permute-start.1 = (bf16[128,512]{1,0:T(8,128)(2,1)}, bf16[128,512]{1,0:T(8,128)(2,1)S(1)}, u32[]{:S(2)}, u32[]{:S(2)}) collective-permute-start(bf16[128,512]{1,0:T(8,128)(2,1)} %param.11), channel_id=1, source_target_pairs={{0,16},{8,24},{16,32},{24,40},{32,48},{40,56},{48,64},{56,72},{64,... | collective-permute-start | bytes 393224 | tf_op jit(solution)/shard_map/ppermute | solution.py:12
  22.0 8.5 %collective-permute-start.2 = (bf16[128,512]{1,0:T(8,128)(2,1)}, bf16[128,512]{1,0:T(8,128)(2,1)S(1)}, u32[]{:S(2)}, u32[]{:S(2)}) collective-permute-start(bf16[128,512]{1,0:T(8,128)(2,1)} %param.11), channel_id=1, source_target_pairs={{0,8},{8,16},{16,24},{24,32},{32,40},{40,48},{48,56},{56,64},{64,7... | collective-permute-start | bytes 393224 | tf_op jit(solution)/shard_map/ppermute | solution.py:12
  25.1 6.3 %collective-permute-start.3 = (bf16[128,512]{1,0:T(8,128)(2,1)}, bf16[128,512]{1,0:T(8,128)(2,1)S(1)}, u32[]{:S(2)}, u32[]{:S(2)}) collective-permute-start(bf16[128,512]{1,0:T(8,128)(2,1)} %param.11), channel_id=1, source_target_pairs={{8,0},{16,8},{24,16},{32,24},{40,32},{48,40},{56,48},{64,56},{72,6... | collective-permute-start | bytes 393224 | tf_op jit(solution)/shard_map/ppermute | solution.py:12
  26.4 11.2 %collective-permute-start.4 = (bf16[128,512]{1,0:T(8,128)(2,1)}, bf16[128,512]{1,0:T(8,128)(2,1)S(1)}, u32[]{:S(2)}, u32[]{:S(2)}) collective-permute-start(bf16[128,512]{1,0:T(8,128)(2,1)} %param.11), channel_id=1, source_target_pairs={{16,0},{24,8},{32,16},{40,24},{48,32},{56,40},{64,48},{72,56},{80,... | collective-permute-start | bytes 393224 | tf_op jit(solution)/shard_map/ppermute | solution.py:12
  29.1 21.6 %collective-permute-start.5 = (bf16[128,512]{1,0:T(8,128)(2,1)}, bf16[128,512]{1,0:T(8,128)(2,1)S(1)}, u32[]{:S(2)}, u32[]{:S(2)}) collective-permute-start(bf16[128,512]{1,0:T(8,128)(2,1)} %param.11), channel_id=1, source_target_pairs={{24,0},{32,8},{40,16},{48,24},{56,32},{64,40},{72,48},{80,56},{88,... | collective-permute-start | bytes 393224 | tf_op jit(solution)/shard_map/ppermute | solution.py:12
  65.1 34.4 %copy-start.3 = (bf16[128,512]{1,0:T(8,128)(2,1)S(1)}, bf16[128,512]{1,0:T(8,128)(2,1)}, u32[]{:S(2)}) copy-start(bf16[128,512]{1,0:T(8,128)(2,1)} %param.17) | copy-start | bytes 393220
  65.1 34.4 %copy-start.4 = (f32[512]{0:T(512)S(1)}, f32[512]{0:T(512)}, u32[]{:S(2)}) copy-start(f32[512]{0:T(512)} %param.13) | copy-start | bytes 6148
  65.1 67.5 %all-gather.2.cloned.1.call-start = ((), (), s32[]{:S(2)}) async-start(), calls=%async_computation.4 | async-start | bytes 1179648 | tf_op jit(solution)/shard_map/all_gather | solution.py:81
  99.5 3.2 copy-start.2
  101.6 31.1 %copy-start.1 = (bf16[16,128,128]{2,1,0:T(8,128)(2,1)S(1)}, bf16[16,128,128]{2,1,0:T(8,128)(2,1)}, u32[]{:S(2)}) copy-start(bf16[16,128,128]{2,1,0:T(8,128)(2,1)} %get-tuple-element.502) | copy-start | bytes 1572868
  102.6 228.5 %all-reduce.3.cloned.1.call-start = ((), (), s32[]{:S(2)}) async-start(), calls=%async_computation.2 | async-start | bytes 2097152 | tf_op jit(solution)/shard_map/psum | solution.py:77
  104.0 387.3 %all-reduce.5.cloned.1.call-start = ((), (), s32[]{:S(2)}) async-start(), calls=%async_computation.3 | async-start | bytes 2097152 | tf_op jit(solution)/shard_map/psum | solution.py:77
  147.3 13.9 %collective-permute-start.10 = (f32[128,512]{1,0:T(8,128)S(1)}, f32[128,512]{1,0:T(8,128)S(1)}, u32[]{:S(2)}, u32[]{:S(2)}) collective-permute-start(f32[128,512]{1,0:T(8,128)S(1)} %get-tuple-element.334), channel_id=1, source_target_pairs={{0,16},{8,24},{16,32},{24,40},{32,48},{40,56},{48,64},{56,72},{64,... | collective-permute-start | bytes 786440 | tf_op jit(solution)/shard_map/ppermute | solution.py:12
  151.5 337.7 %collective-permute-start.11 = (f32[128,512]{1,0:T(8,128)}, f32[128,512]{1,0:T(8,128)S(1)}, u32[]{:S(2)}, u32[]{:S(2)}) collective-permute-start(f32[128,512]{1,0:T(8,128)} %get-tuple-element.333), channel_id=1, source_target_pairs={{0,24},{8,32},{16,40},{24,48},{32,56},{40,64},{48,72},{56,80},{64,... | collective-permute-start | bytes 786440 | tf_op jit(solution)/shard_map/ppermute | solution.py:12
  157.3 332.0 %collective-permute-start.6 = (f32[128,512]{1,0:T(8,128)}, f32[128,512]{1,0:T(8,128)}, u32[]{:S(2)}, u32[]{:S(2)}) collective-permute-start(f32[128,512]{1,0:T(8,128)} %get-tuple-element.332), channel_id=1, source_target_pairs={{24,0},{32,8},{40,16},{48,24},{56,32},{64,40},{72,48},{80,56},{88,... | collective-permute-start | bytes 786440 | tf_op jit(solution)/shard_map/ppermute | solution.py:12
  158.6 330.7 %collective-permute-start.7 = (f32[128,512]{1,0:T(8,128)}, f32[128,512]{1,0:T(8,128)}, u32[]{:S(2)}, u32[]{:S(2)}) collective-permute-start(f32[128,512]{1,0:T(8,128)} %get-tuple-element.337), channel_id=1, source_target_pairs={{16,0},{24,8},{32,16},{40,24},{48,32},{56,40},{64,48},{72,56},{80,... | collective-permute-start | bytes 786440 | tf_op jit(solution)/shard_map/ppermute | solution.py:12
  159.9 329.4 %collective-permute-start.8 = (f32[128,512]{1,0:T(8,128)S(1)}, f32[128,512]{1,0:T(8,128)}, u32[]{:S(2)}, u32[]{:S(2)}) collective-permute-start(f32[128,512]{1,0:T(8,128)S(1)} %get-tuple-element.336), channel_id=1, source_target_pairs={{8,0},{16,8},{24,16},{32,24},{40,32},{48,40},{56,48},{64,56},{72,6... | collective-permute-start | bytes 786440 | tf_op jit(solution)/shard_map/ppermute | solution.py:12
  161.2 328.1 %collective-permute-start.9 = (f32[128,512]{1,0:T(8,128)S(1)}, f32[128,512]{1,0:T(8,128)}, u32[]{:S(2)}, u32[]{:S(2)}) collective-permute-start(f32[128,512]{1,0:T(8,128)S(1)} %get-tuple-element.335), channel_id=1, source_target_pairs={{0,8},{8,16},{16,24},{24,32},{32,40},{40,48},{48,56},{56,64},{64,7... | collective-permute-start | bytes 786440 | tf_op jit(solution)/shard_map/ppermute | solution.py:12
Sparse Core Ops, SparseCore 0:
  65.3 34.1 reduce-scatter.1
  102.7 29.9 all-gather.1
  136.4 194.6 all-reduce.2
  333.4 71.9 all-reduce.4
